TPU v7x, 256 devices: a whole 4x4x8 slice. The times are simulated.
256 devices in a mesh: qa: 8 (over y_lo, x), qb: 32 (over y_hi, z, core).
Axes of the slice: x: 4, y: 4 (y_hi: 2, y_lo: 2; y = y_hi * 2 + y_lo), z: 8, core: 2. Of those that a mesh axis runs over, the one named last changes fastest.
Arguments:
- amplitudes: float32 [2, 16777216], P(None, ('qa', 'qb')), may hold values from -6 to 6
- gate_blocks: float32 [4, 6, 2, 128, 128], replicated, may hold values from -0.375 to 0.375
- phase_low: float32 [4, 256], replicated, may hold values from -3.140625 to 3.140625
- phase_high: float32 [4, 256], replicated, may hold values from -3.140625 to 3.140625
- phase_global: float32 [4, 8, 32], P(None, 'qa', 'qb'), may hold values from -3.140625 to 3.140625
Outputs:
- final_state: float32 [2, 16777216], P(None, ('qa', 'qb'))
All inputs are finite; a program needn't handle non-finite values.
Results may differ from a plain program's by a relative error of at most 0.00011.
Values sent between devices are 32-bit elements; how exact they have to be, the bound alone decides.
A program may use at most 64 MiB of HBM per device.

v0:
```python
import jax
import jax.numpy as jnp
from jax import lax
from jax.sharding import PartitionSpec as P


def apply_gate(state, matrix, where):
    width = matrix.shape[-1]
    cells = state.shape[2]
    stacked = jnp.concatenate([matrix[0], matrix[1]], axis=0)
    if where == 0:
        values = state.reshape(2 * (cells // width), width)
        product = lax.dot_general(
            values, stacked, (((1,), (1,)), ((), ())), precision=lax.Precision.HIGHEST
        )
        product = product.reshape(2, cells // width, 2, width)
        out_real = product[0, :, 0] - product[1, :, 1]
        out_imag = product[0, :, 1] + product[1, :, 0]
    elif where == 1:
        upper = cells // (width * width)
        values = state.reshape(2, upper, width, width)
        product = lax.dot_general(
            stacked, values, (((1,), (2,)), ((), ())), precision=lax.Precision.HIGHEST
        )
        product = product.reshape(2, width, 2, upper, width)
        out_real = jnp.transpose(product[0, :, 0] - product[1, :, 1], (1, 0, 2))
        out_imag = jnp.transpose(product[1, :, 0] + product[0, :, 1], (1, 0, 2))
    else:
        values = state.reshape(2, width, cells // width)
        product = lax.dot_general(
            stacked, values, (((1,), (1,)), ((), ())), precision=lax.Precision.HIGHEST
        )
        product = product.reshape(2, width, 2, cells // width)
        out_real = product[0, :, 0] - product[1, :, 1]
        out_imag = product[1, :, 0] + product[0, :, 1]
    return jnp.stack([out_real.reshape(cells), out_imag.reshape(cells)]).reshape(2, 1, cells)


def apply_phase(state, low_angles, high_angles, global_angles):
    local = (high_angles[:, None] + low_angles[None, :]).reshape(-1)
    theta = global_angles.reshape(-1, 1) + local[None, :]
    cosine = jnp.cos(theta)
    sine = jnp.sin(theta)
    return jnp.stack([state[0] * cosine - state[1] * sine, state[0] * sine + state[1] * cosine])


def regroup_with_gate(state, which, matrix):
    cells = state.shape[2]
    width = matrix.shape[-1]

    def lowest_gate(pieces):
        shape = pieces.shape
        flat = pieces.reshape(2, 1, shape[1] * shape[2] * shape[3])
        return apply_gate(flat, matrix, 0).reshape(shape)

    if which == 0:
        count = lax.axis_size("qa")
        blocks = state.reshape(2, count, cells // (count * width), width)
        moved = lowest_gate(lax.all_to_all(blocks, "qa", split_axis=1, concat_axis=1, tiled=True))
    else:
        count = lax.axis_size("qb")
        blocks = state.reshape(2, count, cells // (count * width), width)
        moved = lowest_gate(lax.all_to_all(blocks, "qb", split_axis=1, concat_axis=1, tiled=True))
    return moved.reshape(2, 1, cells)


def body(amplitudes, gate_blocks, phase_low, phase_high, phase_global):
    cells = amplitudes.shape[1]
    state = amplitudes.reshape(2, 1, cells)
    segments = gate_blocks.shape[0]
    per_segment = gate_blocks.shape[1]
    done_lowest = False
    for segment in range(segments):
        for gate in range(per_segment):
            if gate == 0 and done_lowest:
                continue
            state = apply_gate(state, gate_blocks[segment, gate], gate % 3)
        done_lowest = False
        state = apply_phase(
            state, phase_low[segment], phase_high[segment], phase_global[segment].reshape(1)
        )
        if segment < 3:
            which = 1 if segment == 1 else 0
            state = regroup_with_gate(state, which, gate_blocks[segment + 1, 0])
            done_lowest = True
    return state.reshape(2, cells)


def solution(mesh):
    return jax.shard_map(
        body,
        mesh=mesh,
        in_specs=(P(None, ("qa", "qb")), P(), P(), P(), P(None, "qa", "qb")),
        out_specs=P(None, ("qa", "qb")),
        check_vma=False,
    )
```

profile of v0, /device:TPU:1, one launch (start us, length us, event | category | flops | bytes accessed | tf_op | source)
XLA Modules:
  0.0 104.4 jit_solution(10410167867592833478)
XLA Ops:
  0.0 2.2 %slice_bitcast_fusion.3 = (f32[128,128]{1,0:T(8,128)S(1)}, f32[128,128]{1,0:T(8,128)S(1)}, f32[128,128]{1,0:T(8,128)S(1)}, f32[128,128]{1,0:T(8,128)S(1)}, f32[1...) fusion(f32[4,6,2,128,128]{4,3,2,1,0:T(8,128)} %param.6), kind=kLoop, calls=%fused_computation.214 | loop fusion | bytes 2490368 | tf_op jit(solution)/shard_map/squeeze | solution.py:10
  2.2 2.1 %slice_bitcast_fusion.21 = (f32[128,128]{1,0:T(8,128)}, f32[128,128]{1,0:T(8,128)}, f32[128,128]{1,0:T(8,128)}, f32[128,128]{1,0:T(8,128)S(1)}, f32[128,128]{1,0...) fusion(f32[4,6,2,128,128]{4,3,2,1,0:T(8,128)} %param.6), kind=kLoop, calls=%fused_computation.232 | loop fusion | bytes 2490368 | tf_op jit(solution)/shard_map/squeeze | solution.py:10
  4.3 0.5 reshape_reshape.2
  4.8 1.9 %convolution_bitcast_fusion = f32[1024,256]{0,1:T(8,128)S(1)} fusion(f32[1024,128]{1,0:T(8,128)S(1)} %reshape_reshape.2, f32[128,128]{1,0:T(8,128)} %get-tuple-element.20, f32[128,128]{1,0:T(8,128)} %get-tuple-element.21), kind=kOutput, calls=%fused_computation | convolution fusion | flops 402685952 | bytes 1703936 | tf_op jit(solution)/shard_map/dot_general | solution.py:13
  6.6 0.9 reshape.1369
  7.5 0.5 slice_subtract_fusion.23
  8.4 1.0 pad_maximum_fusion.17
  9.3 1.0 fusion
  10.5 1.0 fusion.3
  11.8 1.0 fusion.6
  12.9 1.0 fusion.9
  14.1 1.0 fusion.12
  15.5 0.7 fusion.117
  16.2 1.8 %fusion.82 = (f32[1,8,64,128]{3,2,0,1:T(8,128)S(1)}, f32[1,8,64,128]{3,2,0,1:T(8,128)S(1)}) fusion(f32[1,8,64,128]{3,2,1,0:T(8,128)S(1)} %add.638, f32[1,8,64,128]{3,2,1,0:T(8,128)S(1)} %sub.368, f32[64,128]{1,0:T(8,128)S(1)} %bitcast.579, f32[8,64]{1,0:T(8,128)S(1)} %copy.27, f32[]{:T(128)} %bitcast.106), kind=kLoop, calls=%fused_computation.169 | loop fusion | flops 524288 | bytes 1083396 | tf_op jit(solution)/shard_map/sub | solution.py:44
  18.0 0.8 pad_maximum_fusion
  18.9 5.9 %all-to-all-start = ((f32[2,8,64,128]{3,2,0,1:T(8,128)}), f32[2,8,64,128]{3,2,0,1:T(8,128)S(1)}, u32[]{:S(2)}, u32[]{:S(2)}) async-start(f32[2,8,64,128]{3,2,0,1:T(8,128)} %pad_maximum_fusion), calls=%async_computation | async-start | bytes 1048576 | tf_op jit(solution)/shard_map/all_to_all | solution.py:59
  25.1 9.9 %all-to-all-done = f32[2,8,64,128]{3,2,0,1:T(8,128)S(1)} async-done(((f32[2,8,64,128]{3,2,0,1:T(8,128)}), f32[2,8,64,128]{3,2,0,1:T(8,128)S(1)}, u32[]{:S(2)}, u32[]{:S(2)}) %all-to-all-start) | async-done | bytes 524320 | tf_op jit(solution)/shard_map/all_to_all | solution.py:59
  35.0 1.0 fusion.118
  36.0 1.0 fusion.15
  37.2 1.0 fusion.18
  38.3 1.0 fusion.21
  39.4 1.0 fusion.24
  40.5 1.0 fusion.27
  41.7 1.7 %fusion.80 = (f32[1,32,16,128]{3,2,0,1:T(8,128)S(1)}, f32[1,32,16,128]{3,2,0,1:T(8,128)S(1)}) fusion(f32[1,32,16,128]{3,2,1,0:T(8,128)S(1)} %add.663, f32[1,32,16,128]{3,2,1,0:T(8,128)S(1)} %sub.381, f32[16,128]{1,0:T(8,128)S(1)} %bitcast.582, f32[32,16]{1,0:T(8,128)S(1)} %copy.34, f32[]{:T(128)} %bitcast.143), kind=kLoop, calls=%fused_computation.163 | loop fusion | flops 524288 | bytes 1058820 | tf_op jit(solution)/shard_map/sub | solution.py:44
  43.4 0.8 pad_maximum_fusion.1
  44.2 11.8 %all-to-all-start.1 = ((f32[2,32,16,128]{3,2,0,1:T(8,128)}), f32[2,32,16,128]{3,2,0,1:T(8,128)S(1)}, u32[]{:S(2)}, u32[]{:S(2)}) async-start(f32[2,32,16,128]{3,2,0,1:T(8,128)} %pad_maximum_fusion.1), calls=%async_computation.1 | async-start | bytes 1048576 | tf_op jit(solution)/shard_map/all_to_all | solution.py:63
  56.3 1.6 %fusion.84 = (f32[256,256]{1,0:T(8,128)S(1)}, f32[256,256]{1,0:T(8,128)S(1)}) fusion(f32[256]{0:T(256)S(1)} %bitcast.585, f32[256]{0:T(256)S(1)} %bitcast.584, f32[]{:T(128)} %bitcast.217), kind=kLoop, calls=%fused_computation.174 | loop fusion | flops 131072 | bytes 526340 | tf_op jit(solution)/shard_map/sin | solution.py:43
  58.6 1.2 %slice_bitcast_fusion.41 = (f32[128,128]{1,0:T(8,128)S(1)}, f32[128,128]{1,0:T(8,128)S(1)}, f32[128,128]{1,0:T(8,128)S(1)}, f32[128,128]{1,0:T(8,128)S(1)}, f32[...) fusion(f32[4,6,2,128,128]{4,3,2,1,0:T(8,128)} %param.6), kind=kLoop, calls=%fused_computation.252 | loop fusion | bytes 1310720 | tf_op jit(solution)/shard_map/squeeze | solution.py:10
  59.7 14.4 %all-to-all-done.1 = f32[2,32,16,128]{3,2,0,1:T(8,128)S(1)} async-done(((f32[2,32,16,128]{3,2,0,1:T(8,128)}), f32[2,32,16,128]{3,2,0,1:T(8,128)S(1)}, u32[]{:S(2)}, u32[]{:S(2)}) %all-to-all-start.1) | async-done | bytes 524320 | tf_op jit(solution)/shard_map/all_to_all | solution.py:63
  74.2 1.0 fusion.119
  75.2 1.0 fusion.30
  76.4 1.0 fusion.33
  77.5 1.0 fusion.36
  78.5 1.0 fusion.39
  79.7 1.0 fusion.42
  80.9 1.9 %fusion.78 = (f32[1,8,64,128]{3,2,0,1:T(8,128)S(1)}, f32[1,8,64,128]{3,2,0,1:T(8,128)S(1)}) fusion(f32[1,8,64,128]{3,2,1,0:T(8,128)S(1)} %add.688, f32[1,8,64,128]{3,2,1,0:T(8,128)S(1)} %sub.394, f32[64,128]{1,0:T(8,128)S(1)} %bitcast.578, f32[8,64]{1,0:T(8,128)S(1)} %copy.41, f32[]{:T(128)} %bitcast.180), kind=kLoop, calls=%fused_computation.157 | loop fusion | flops 524288 | bytes 1083396 | tf_op jit(solution)/shard_map/sub | solution.py:44
  82.7 0.8 pad_maximum_fusion.2
  83.6 3.8 %all-to-all-start.2 = ((f32[2,8,64,128]{3,2,0,1:T(8,128)}), f32[2,8,64,128]{3,2,0,1:T(8,128)S(1)}, u32[]{:S(2)}, u32[]{:S(2)}) async-start(f32[2,8,64,128]{3,2,0,1:T(8,128)} %pad_maximum_fusion.2), calls=%async_computation.2 | async-start | bytes 1048576 | tf_op jit(solution)/shard_map/all_to_all | solution.py:59
  87.4 7.8 %all-to-all-done.2 = f32[2,8,64,128]{3,2,0,1:T(8,128)S(1)} async-done(((f32[2,8,64,128]{3,2,0,1:T(8,128)}), f32[2,8,64,128]{3,2,0,1:T(8,128)S(1)}, u32[]{:S(2)}, u32[]{:S(2)}) %all-to-all-start.2) | async-done | bytes 524320 | tf_op jit(solution)/shard_map/all_to_all | solution.py:59
  95.3 1.0 fusion.120
  96.3 1.0 fusion.45
  97.5 1.0 fusion.48
  98.6 1.0 fusion.51
  99.7 1.0 fusion.54
  100.8 1.0 fusion.57
  102.2 0.3 sub.407
  102.5 0.5 fusion.76
  103.1 1.3 %maximum_bitcast_fusion.40 = f32[2,65536]{1,0:T(2,128)} fusion(f32[1,1,65536]{2,0,1:T(1,128)S(1)} %get-tuple-element.57, f32[1,1,65536]{2,0,1:T(1,128)S(1)} %get-tuple-element.56), kind=kLoop, calls=%fused_computation.84 | loop fusion | flops 131072 | bytes 1048576 | tf_op jit(solution)/shard_map/reshape | solution.py:86
  (119 shorter events, 4.7 us)
Async XLA Ops:
  0.0 4.3 %copy-start = (f32[2,65536]{1,0:T(2,128)S(1)}, f32[2,65536]{1,0:T(2,128)}, u32[]{:S(2)}) copy-start(f32[2,65536]{1,0:T(2,128)} %param.5) | copy-start | bytes 1572868
  10.3 1.4 %copy-start.7 = (f32[128,128]{1,0:T(8,128)S(1)}, f32[128,128]{1,0:T(8,128)}, u32[]{:S(2)}) copy-start(f32[128,128]{1,0:T(8,128)} %get-tuple-element.14) | copy-start | bytes 196612
  10.3 1.4 %copy-start.8 = (f32[128,128]{1,0:T(8,128)S(1)}, f32[128,128]{1,0:T(8,128)}, u32[]{:S(2)}) copy-start(f32[128,128]{1,0:T(8,128)} %get-tuple-element.15) | copy-start | bytes 196612
  10.3 1.4 %copy-start.9 = (f32[128,128]{1,0:T(8,128)S(1)}, f32[128,128]{1,0:T(8,128)}, u32[]{:S(2)}) copy-start(f32[128,128]{1,0:T(8,128)} %get-tuple-element.18) | copy-start | bytes 196612
  10.4 1.4 %copy-start.10 = (f32[128,128]{1,0:T(8,128)S(1)}, f32[128,128]{1,0:T(8,128)}, u32[]{:S(2)}) copy-start(f32[128,128]{1,0:T(8,128)} %get-tuple-element.19) | copy-start | bytes 196612
  11.5 1.3 %copy-start.3 = (f32[128,128]{1,0:T(8,128)S(1)}, f32[128,128]{1,0:T(8,128)}, u32[]{:S(2)}) copy-start(f32[128,128]{1,0:T(8,128)} %get-tuple-element.26) | copy-start | bytes 196612
  11.5 1.3 %copy-start.4 = (f32[128,128]{1,0:T(8,128)S(1)}, f32[128,128]{1,0:T(8,128)}, u32[]{:S(2)}) copy-start(f32[128,128]{1,0:T(8,128)} %get-tuple-element.27) | copy-start | bytes 196612
  11.5 1.3 %copy-start.5 = (f32[128,128]{1,0:T(8,128)S(1)}, f32[128,128]{1,0:T(8,128)}, u32[]{:S(2)}) copy-start(f32[128,128]{1,0:T(8,128)} %get-tuple-element.28) | copy-start | bytes 196612
  11.6 1.3 %copy-start.6 = (f32[128,128]{1,0:T(8,128)S(1)}, f32[128,128]{1,0:T(8,128)}, u32[]{:S(2)}) copy-start(f32[128,128]{1,0:T(8,128)} %get-tuple-element.29) | copy-start | bytes 196612
  13.9 1.4 %copy-start.12 = (f32[4,256]{1,0:T(4,128)S(1)}, f32[4,256]{1,0:T(4,128)}, u32[]{:S(2)}) copy-start(f32[4,256]{1,0:T(4,128)} %param.8) | copy-start | bytes 12292
  14.0 1.6 %copy-start.13 = (f32[4,256]{1,0:T(4,128)S(1)}, f32[4,256]{1,0:T(4,128)}, u32[]{:S(2)}) copy-start(f32[4,256]{1,0:T(4,128)} %param.7) | copy-start | bytes 12292
  14.0 1.6 %copy-start.11 = (f32[4,1,1]{0,2,1:T(1,128)S(1)}, f32[4,1,1]{0,2,1:T(1,128)}, u32[]{:S(2)}) copy-start(f32[4,1,1]{0,2,1:T(1,128)} %param.9) | copy-start | bytes 52
  15.1 9.9 %copy-start.1 = (f32[128,128]{1,0:T(8,128)S(1)}, f32[128,128]{1,0:T(8,128)}, u32[]{:S(2)}) copy-start(f32[128,128]{1,0:T(8,128)} %get-tuple-element.32) | copy-start | bytes 196612
  15.1 9.9 %copy-start.2 = (f32[128,128]{1,0:T(8,128)S(1)}, f32[128,128]{1,0:T(8,128)}, u32[]{:S(2)}) copy-start(f32[128,128]{1,0:T(8,128)} %get-tuple-element.33) | copy-start | bytes 196612
  18.9 16.1 %all-to-all-start = ((f32[2,8,64,128]{3,2,0,1:T(8,128)}), f32[2,8,64,128]{3,2,0,1:T(8,128)S(1)}, u32[]{:S(2)}, u32[]{:S(2)}) async-start(f32[2,8,64,128]{3,2,0,1:T(8,128)} %pad_maximum_fusion), calls=%async_computation | async-start | bytes 1048576 | tf_op jit(solution)/shard_map/all_to_all | solution.py:59
  44.2 29.9 %all-to-all-start.1 = ((f32[2,32,16,128]{3,2,0,1:T(8,128)}), f32[2,32,16,128]{3,2,0,1:T(8,128)S(1)}, u32[]{:S(2)}, u32[]{:S(2)}) async-start(f32[2,32,16,128]{3,2,0,1:T(8,128)} %pad_maximum_fusion.1), calls=%async_computation.1 | async-start | bytes 1048576 | tf_op jit(solution)/shard_map/all_to_all | solution.py:63
  83.6 11.7 %all-to-all-start.2 = ((f32[2,8,64,128]{3,2,0,1:T(8,128)}), f32[2,8,64,128]{3,2,0,1:T(8,128)S(1)}, u32[]{:S(2)}, u32[]{:S(2)}) async-start(f32[2,8,64,128]{3,2,0,1:T(8,128)} %pad_maximum_fusion.2), calls=%async_computation.2 | async-start | bytes 1048576 | tf_op jit(solution)/shard_map/all_to_all | solution.py:59
where the time goes:
time: 106 us; the launch traced here: 104 us
  waiting for transfers between devices  32.1 us (30%)
  matrix products  24.5 us (23%)
  starting transfers between devices  21.4 us (20%)
  other arithmetic  14.6 us (14%)
  local copies, waits for them, and re-layouts  10.7 us (10%)
  between operations  1.1 us (1%)
    all_to_all x2, waiting for transfers between devices, regroup_with_gate(): lax.all_to_all(blocks, 'qa', split_axis=1, concat_axis=1, tiled=True)  17.7 us
    all_to_all x1, waiting for transfers between devices, regroup_with_gate(): lax.all_to_all(blocks, 'qb', split_axis=1, concat_axis=1, tiled=True)  14.4 us
    all_to_all x1, starting transfers between devices, regroup_with_gate(): lax.all_to_all(blocks, 'qb', split_axis=1, concat_axis=1, tiled=True)  11.8 us
    all_to_all x2, starting transfers between devices, regroup_with_gate(): lax.all_to_all(blocks, 'qa', split_axis=1, concat_axis=1, tiled=True)  9.62 us
    dot_general x8, matrix products, apply_gate(): lax.dot_general(values, stacked, (((1,), (1,)), ((), ())), precision=lax....  8.77 us
    dot_general x8, matrix products, apply_gate(): lax.dot_general(stacked, values, (((1,), (2,)), ((), ())), precision=lax....  7.85 us
    dot_general x8, matrix products, apply_gate(): lax.dot_general(stacked, values, (((1,), (1,)), ((), ())), precision=lax....  7.84 us
    sub x4, other arithmetic, apply_phase(): state[0] * cosine - state[1] * sine  5.93 us
  transfers between devices with their start and end apart: 3, of which 3 were waited for; matrix products, arithmetic and copies ran while one was open for 4% of the time, Pallas kernels for 0%

commit v1 on v0

v1 whole, which is shorter than its diff:
```python
import jax
import jax.numpy as jnp
from jax import lax
from jax.experimental import pallas as pl
from jax.experimental.pallas import tpu as pltpu
from jax.sharding import PartitionSpec as P

F32, BF16 = jnp.float32, jnp.bfloat16
MESH = pl.DeviceIdType.MESH


def dot(a, b):
    return lax.dot_general(a, b, (((1,), (0,)), ((), ())), preferred_element_type=F32)


def dot_t(a, b):
    return lax.dot_general(a, b, (((1,), (1,)), ((), ())), preferred_element_type=F32)


def parts(x):
    high = x.astype(BF16)
    return high, (x - high.astype(F32)).astype(BF16)


def dot3(wh, wl, x):
    xh, xl = parts(x)
    return dot(wh, xh) + dot(wh, xl) + dot(wl, xh)


def iota(shape, axis):
    return lax.broadcasted_iota(jnp.int32, shape, axis)


def half_swap(x, y):
    low = iota(x.shape, 1) < 64
    xr, yr = pltpu.roll(x, 64, 1), pltpu.roll(y, 64, 1)
    return jnp.where(low, x, yr), jnp.where(low, xr, y)


def other_part(x):
    tiles = x.reshape(x.shape[0] // 8, 8, x.shape[1])
    return pltpu.roll(tiles, 4, 1).reshape(x.shape)


def part_sign(shape):
    return jnp.where((iota(shape, 0) // 4) % 2 == 0, -1.0, 1.0).astype(F32)


def embed(re, im):
    return jnp.concatenate(
        [jnp.concatenate([re, -im], axis=1), jnp.concatenate([im, re], axis=1)], axis=0
    )


def kernel(
    amp, gates, p_low, p_high, p_glob, out,
    amp_v, gates_v, low_v, high_v, glob_s, order, wh, wl, bh, bl, full, sends, recvs,
    row_t, mid_t, last_t, in_sem, gate_sem, send_sem, recv_sem,
):
    qa, qb = lax.axis_index("qa"), lax.axis_index("qb")

    gate_copies = [
        pltpu.make_async_copy(
            gates.at[pl.ds(12 * s, 12)], gates_v.at[pl.ds(12 * s, 12)], gate_sem.at[s]
        )
        for s in range(4)
    ]
    amp_copy = pltpu.make_async_copy(amp, amp_v, in_sem.at[0])
    small = [
        pltpu.make_async_copy(p_low, low_v, in_sem.at[1]),
        pltpu.make_async_copy(p_high, high_v, in_sem.at[2]),
        pltpu.make_async_copy(p_glob, glob_s, in_sem.at[3]),
    ]
    gate_copies[0].start()
    amp_copy.start()
    for copy in small:
        copy.start()
    for s in range(1, 4):
        gate_copies[s].start()

    barrier = pltpu.get_barrier_semaphore()

    def greet(axis, me, count):
        def step(i, carry):
            peer = lax.rem(me + i, count)
            pl.semaphore_signal(barrier, inc=1, device_id={axis: peer}, device_id_type=MESH)
            return carry

        lax.fori_loop(1, count, step, 0)

    greet("qa", qa, 8)
    greet("qb", qb, 32)

    p, n = iota((256, 256), 0), iota((256, 256), 1)
    at0 = ((p // 4) % 2) * 128 + ((p // 16) % 8) * 16 + (p % 4) * 4 + ((p // 8) % 2) * 2 + p // 128
    at1 = ((p // 4) % 2) * 128 + (p // 8) * 4 + p % 4
    at2 = (p % 2) * 128 + p // 2
    for i, at in enumerate((at0, at1, at2)):
        order[i] = jnp.where(n == at, 1.0, 0.0).astype(BF16)

    def real_gate(s, g):
        at = (s * 6 + g) * 2
        return embed(gates_v[at], gates_v[at + 1])

    def prepare(s, i, rows, cols):
        h, l = parts(real_gate(s, 1 + i + i // 2))
        if rows is not None:
            both = dot(order[rows], jnp.concatenate([h, l], axis=1)).astype(BF16)
            h, l = both[:, :256], both[:, 256:]
        wh[4 * s + i] = dot_t(h, order[cols]).astype(BF16)
        wl[4 * s + i] = dot_t(l, order[cols]).astype(BF16)

    def prepare_range(s, first, last):
        def step(i, carry):
            prepare(s, i, i % 2, i % 2)
            return carry

        lax.fori_loop(first, last, step, 0)

    def joined_low(s):
        a, b = (s * 6 + 3) * 2, s * 12
        ah, al = parts(embed(gates_v[a], gates_v[a + 1]))
        return dot3(ah, al, jnp.concatenate([gates_v[b], gates_v[b + 1]], axis=0))

    def prepare_low(slot, s, low_cos, low_sin):
        first, second = joined_low(s), joined_low(s + 1)
        re, im = second[:128], second[128:]
        for b7 in range(2):
            co = low_cos[s : s + 1, 128 * b7 : 128 * b7 + 128]
            si = low_sin[s : s + 1, 128 * b7 : 128 * b7 + 128]
            ah, al = parts(embed(re * co - im * si, re * si + im * co))
            h, l = parts(dot3(ah, al, first))
            bh[slot, b7] = jnp.concatenate([h, h], axis=1)
            bl[slot, b7] = l

    def apply_low(slot, b7, x):
        xh, xl = parts(x)
        y = dot_t(jnp.concatenate([xh, xl], axis=1), bh[slot, b7]) + dot_t(xh, bl[slot, b7])
        return y[:, :128] + part_sign((512, 128)) * other_part(y[:, 128:])

    def expand(one_hot, co, si):
        lanes = jnp.concatenate(
            [jnp.broadcast_to(co, (128, 256)), jnp.broadcast_to(si, (128, 256))], axis=0
        )
        h, l = parts(lanes)
        both = dot_t(one_hot, h) + dot_t(one_hot, l)
        return both[:, :128], both[:, 128:]

    def row_one_hot():
        r, c = iota((512, 256), 0), iota((512, 256), 1)
        at = ((r // 16) * 4 + r % 4) * 2 + (r // 8) % 2
        return jnp.where(c == at, 1.0, 0.0).astype(BF16)

    def turn(x, table, at):
        return x * table[at, 0] + other_part(x) * table[at, 1]

    def full_middle(w, src):
        x = jnp.concatenate(
            [
                jnp.concatenate([src[b7, u * 128 : u * 128 + 128] for b7 in range(2)], axis=0)
                for u in range(4)
            ],
            axis=1,
        )
        y = dot3(wh[w], wl[w], x)
        for u in range(4):
            for b7 in range(2):
                full[b7, u * 128 : u * 128 + 128] = y[
                    128 * b7 : 128 * b7 + 128, 128 * u : 128 * u + 128
                ]

    def columns(x):
        x = x.reshape(32, 2, 8, 128)
        return jnp.concatenate([x[:, b8].reshape(256, 128) for b8 in range(2)], axis=1)

    def rows_again(y):
        halves = [y[:, 128 * b8 : 128 * b8 + 128].reshape(32, 1, 8, 128) for b8 in range(2)]
        return jnp.concatenate(halves, axis=1).reshape(512, 128)

    def top_gate(w, x):
        return rows_again(dot3(wh[w], wl[w], columns(x)))

    def full_top(w):
        x = jnp.concatenate([columns(full[b7]) for b7 in range(2)], axis=1)
        y = dot3(wh[w], wl[w], x)
        for b7 in range(2):
            full[b7] = rows_again(y[:, 256 * b7 : 256 * b7 + 256])

    def middle_gate(w, x):
        a, b = half_swap(x[:256], x[256:])
        x = jnp.concatenate(
            [
                jnp.concatenate([a[128 * u : 128 * u + 128], b[128 * u : 128 * u + 128]], axis=0)
                for u in range(2)
            ],
            axis=1,
        )
        y = dot3(wh[w], wl[w], x)
        a = jnp.concatenate([y[:128, :128], y[:128, 128:]], axis=0)
        b = jnp.concatenate([y[128:, :128], y[128:, 128:]], axis=0)
        return jnp.concatenate(half_swap(a, b), axis=0)

    def start(stage, k, axis, me, count):
        size = 512 // count

        def step(i, carry):
            peer = lax.rem(me + i, count)
            pltpu.make_async_remote_copy(
                src_ref=sends.at[stage, k, pl.ds(pl.multiple_of(peer * size, size), size)],
                dst_ref=recvs.at[stage, k, pl.ds(pl.multiple_of(me * size, size), size)],
                send_sem=send_sem.at[stage, k],
                recv_sem=recv_sem.at[stage, k],
                device_id={axis: peer},
                device_id_type=MESH,
            ).start()
            return carry

        lax.fori_loop(1, count, step, 0)
        own = pl.ds(pl.multiple_of(me * size, size), size)
        recvs[stage, k, own, :] = sends[stage, k, own, :]

    def finish(bufs, sem, stage, k, count):
        moved = 512 - 512 // count
        view = bufs.at[stage, k, pl.ds(0, moved)]
        pltpu.make_async_copy(view, view, sem.at[stage, k]).wait()

    gate_copies[0].wait()
    prepare(0, 0, 0, 2)
    prepare_range(0, 1, 4)
    amp_copy.wait()
    x = jnp.concatenate([amp_v[256 * u : 256 * u + 256, :] for u in range(4)], axis=1)
    y = dot3(wh[0], wl[0], x)
    for u in range(4):
        for b7 in range(2):
            full[b7, u * 128 : u * 128 + 128] = y[
                128 * b7 : 128 * b7 + 128, 128 * u : 128 * u + 128
            ]
    full_top(1)
    full_middle(2, full)

    for copy in small:
        copy.wait()
    low_cos, low_sin = jnp.cos(low_v[...]), jnp.sin(low_v[...])
    seg = iota((4, 256), 0)
    glob = jnp.zeros((4, 256), F32)
    for s in range(4):
        glob = jnp.where(seg == s, glob_s[s, 0, 0], glob)
    row_cos, row_sin = jnp.cos(high_v[...] + glob), jnp.sin(high_v[...] + glob)

    def row_table(s):
        c, t = expand(row_one_hot(), row_cos[s : s + 1], row_sin[s : s + 1])
        row_t[s, 0] = c
        row_t[s, 1] = part_sign((512, 128)) * t

    row_table(0)
    gate_copies[1].wait()
    prepare_low(0, 0, low_cos, low_sin)
    a, b = half_swap(apply_low(0, 0, full[0]), apply_low(0, 1, full[1]))
    full[0] = a
    full[1] = b
    pl.semaphore_wait(barrier, 38)

    def leave0(k, carry):
        sends[0, k] = turn(top_gate(3, full[k]), row_t, 0)
        start(0, k, "qa", qa, 8)
        return carry

    lax.fori_loop(0, 2, leave0, 0)

    prepare_range(1, 0, 4)
    row_table(1)
    v, w = half_swap(
        jnp.broadcast_to(low_cos[1:2, :128], (8, 128)), jnp.broadcast_to(low_cos[1:2, 128:], (8, 128))
    )
    vs, ws = half_swap(
        jnp.broadcast_to(low_sin[1:2, :128], (8, 128)), jnp.broadcast_to(low_sin[1:2, 128:], (8, 128))
    )
    for k, (co, si) in enumerate(((v, vs), (w, ws))):
        co, si = co[:1], si[:1]
        sign = part_sign((512, 128))
        mid_t[k, 0] = row_t[1, 0] * co - row_t[1, 1] * sign * si
        mid_t[k, 1] = row_t[1, 1] * co + row_t[1, 0] * sign * si

    def between(k, carry):
        finish(recvs, recv_sem, 0, k, 8)
        x = middle_gate(4, recvs[0, k])
        x = top_gate(5, x)
        x = middle_gate(6, x)
        x = top_gate(7, x)
        sends[1, k] = turn(x, mid_t, k)
        start(1, k, "qb", qb, 32)
        return carry

    lax.fori_loop(0, 2, between, 0)

    gate_copies[2].wait()
    gate_copies[3].wait()
    prepare_range(2, 0, 4)
    prepare_range(3, 0, 3)
    prepare(3, 3, None, 1)
    prepare_low(1, 2, low_cos, low_sin)
    row_table(2)
    r, c = iota((256, 256), 0), iota((256, 256), 1)
    one_hot = jnp.where(c == (r % 128) * 2 + r // 128, 1.0, 0.0).astype(BF16)
    co3, si3 = expand(one_hot, row_cos[3:4], row_sin[3:4])
    for b8 in range(2):
        rc, rs = co3[128 * b8 : 128 * b8 + 128], si3[128 * b8 : 128 * b8 + 128]
        for b7 in range(2):
            lc = low_cos[3:4, 128 * b7 : 128 * b7 + 128]
            ls = low_sin[3:4, 128 * b7 : 128 * b7 + 128]
            last_t[b8, b7, 0] = rc * lc - rs * ls
            last_t[b8, b7, 1] = rs * lc + rc * ls

    def arrive1(k, carry):
        finish(recvs, recv_sem, 1, k, 32)
        x = middle_gate(8, recvs[1, k])
        x = top_gate(9, x)
        full[k] = middle_gate(10, x)
        return carry

    lax.fori_loop(0, 2, arrive1, 0)
    a, b = half_swap(full[0], full[1])
    full[0] = a
    full[1] = b

    def leave2(b7, carry):
        x = apply_low(1, b7, full[b7])
        sends[2, b7] = turn(top_gate(11, x), row_t, 2)
        start(2, b7, "qa", qa, 8)
        return carry

    lax.fori_loop(0, 2, leave2, 0)

    for b7 in range(2):
        finish(recvs, recv_sem, 2, b7, 8)
    full_middle(12, recvs.at[2])
    full_top(13)
    full_middle(14, full)
    for b7 in range(2):
        y = dot3(wh[15], wl[15], columns(full[b7]))
        for b8 in range(2):
            re = y[:128, 128 * b8 : 128 * b8 + 128]
            im = y[128:, 128 * b8 : 128 * b8 + 128]
            co, si = last_t[b8, b7, 0], last_t[b8, b7, 1]
            at = 4 * b8 + 2 * b7
            out[pl.ds(at, 128, stride=8), :] = re * co - im * si
            out[pl.ds(at + 1, 128, stride=8), :] = im * co + re * si

    for stage, count in ((0, 8), (1, 32), (2, 8)):
        for k in range(2):
            finish(sends, send_sem, stage, k, count)


def body(amplitudes, gate_blocks, phase_low, phase_high, phase_global):
    cells = amplitudes.shape[1]
    rows = cells // 128
    amp = amplitudes.reshape(2, rows, 128).transpose(1, 0, 2).reshape(2 * rows, 128)
    anywhere = pl.BlockSpec(memory_space=pl.ANY)
    result = pl.pallas_call(
        kernel,
        name="circuit",
        out_shape=jax.ShapeDtypeStruct((2 * rows, 128), F32),
        in_specs=[anywhere] * 5,
        out_specs=pl.BlockSpec(memory_space=pltpu.VMEM),
        scratch_shapes=[
            pltpu.VMEM((1024, 128), F32),
            pltpu.VMEM((48, 128, 128), F32),
            pltpu.VMEM((4, 256), F32),
            pltpu.VMEM((4, 256), F32),
            pltpu.SMEM((4, 1, 1), F32),
            pltpu.VMEM((3, 256, 256), BF16),
            pltpu.VMEM((16, 256, 256), BF16),
            pltpu.VMEM((16, 256, 256), BF16),
            pltpu.VMEM((2, 2, 256, 256), BF16),
            pltpu.VMEM((2, 2, 256, 128), BF16),
            pltpu.VMEM((2, 512, 128), F32),
            pltpu.VMEM((3, 2, 512, 128), F32),
            pltpu.VMEM((3, 2, 512, 128), F32),
            pltpu.VMEM((3, 2, 512, 128), F32),
            pltpu.VMEM((2, 2, 512, 128), F32),
            pltpu.VMEM((2, 2, 2, 128, 128), F32),
            pltpu.SemaphoreType.DMA((4,)),
            pltpu.SemaphoreType.DMA((4,)),
            pltpu.SemaphoreType.DMA((3, 2)),
            pltpu.SemaphoreType.DMA((3, 2)),
        ],
        compiler_params=pltpu.CompilerParams(
            collective_id=0, has_side_effects=True, vmem_limit_bytes=40 << 20
        ),
    )(amp, gate_blocks.reshape(48, 128, 128), phase_low, phase_high, phase_global)
    return result.reshape(rows, 2, 128).transpose(1, 0, 2).reshape(2, cells)


def solution(mesh):
    return jax.shard_map(
        body,
        mesh=mesh,
        in_specs=(P(None, ("qa", "qb")), P(), P(), P(), P(None, "qa", "qb")),
        out_specs=P(None, ("qa", "qb")),
        check_vma=False,
    )
```

time: 106 us -> 51.4 us (0.48); the launches traced: 104 us -> 51.1 us
  Pallas kernels: 0 us -> 45.3 us
  waiting for transfers between devices: 32.1 us -> 0 us
  matrix products: 24.5 us -> 0 us
  starting transfers between devices: 21.4 us -> 0 us
  other arithmetic: 14.6 us -> 0 us
  local copies, waits for them, and re-layouts: 10.7 us -> 5.84 us
  between operations: 1.1 us -> 0.01 us
    pallas_call x0 -> x1, Pallas kernels: none -> 45.3 us  [body(): pl.pallas_call(kernel, name='circuit', out_shape=jax.ShapeDtypeStruct((2...]
    all_to_all x3 -> x0, waiting for transfers between devices: 32.1 us -> none  [the longest x2 17.7 us: regroup_with_gate(): lax.all_to_all(blocks, 'qa', split_axis=1, concat_axis=1, tiled=True)]
    dot_general x24 -> x0, matrix products: 24.5 us -> none  [the longest x8 8.77 us: apply_gate(): lax.dot_general(values, stacked, (((1,), (1,)), ((), ())), precision=lax....]
    all_to_all x3 -> x0, starting transfers between devices: 21.4 us -> none  [the longest x1 11.8 us: regroup_with_gate(): lax.all_to_all(blocks, 'qb', split_axis=1, concat_axis=1, tiled=True)]
    sub x20 -> x0, other arithmetic: 7.52 us -> none  [the longest x4 5.93 us: apply_phase(): state[0] * cosine - state[1] * sine]
    unnamed x28 -> x10, local copies, waits for them, and re-layouts: 0.07 us -> 5.84 us
    squeeze x3 -> x0, local copies, waits for them, and re-layouts: 5.48 us -> none  [apply_gate(): stacked = jnp.concatenate([matrix[0], matrix[1]], axis=0)]
    another operation x3 -> x0, other arithmetic: 2.5 us -> none  [apply_phase(): jnp.stack([state[0] * cosine - state[1] * sine, state[0] * sine + state[1...]
  transfers between devices with their start and end apart: 3 -> 0, of which waited for: 3 -> 0; matrix products, arithmetic and copies ran while one was open for 4% -> 0% of each run, Pallas kernels for 0% -> 0%
where the time goes in v1:
time: 51.4 us; the launch traced here: 51.1 us
  Pallas kernels  45.3 us (88%)
  local copies, waits for them, and re-layouts  5.84 us (11%)
    pallas_call x1, Pallas kernels, body(): pl.pallas_call(kernel, name='circuit', out_shape=jax.ShapeDtypeStruct((2...  45.3 us
    unnamed x10, local copies, waits for them, and re-layouts  5.84 us

profile of v1, /device:TPU:1, one launch (start us, length us, event | category | flops | bytes accessed | tf_op | source)
XLA Modules:
  0.0 51.1 jit_solution(16099965040145931194)
XLA Ops:
  0.0 0.7 %copy.7.p_glob = f32[4,1,1]{2,1,0:T(1,128)S(1)} copy(f32[4,1,1]{0,2,1:T(1,128)} %param.9) | data formatting | bytes 32 | tf_op args[4]
  0.7 0.0 copy-start
  0.7 1.9 %copy-done = f32[4,6,2,128,128]{4,3,2,1,0:T(8,128)S(1)} copy-done((f32[4,6,2,128,128]{4,3,2,1,0:T(8,128)S(1)}, f32[4,6,2,128,128]{4,3,2,1,0:T(8,128)}, u32[]{:S(2)}) %copy-start) | copy-done | bytes 3145752
  2.6 0.0 copy-start.1
  2.6 1.0 %copy-done.1 = f32[2,65536]{1,0:T(2,128)S(1)} copy-done((f32[2,65536]{1,0:T(2,128)S(1)}, f32[2,65536]{1,0:T(2,128)}, u32[]{:S(2)}) %copy-start.1) | copy-done | bytes 524312
  3.7 0.0 copy-start.2
  3.7 0.7 %copy-done.2 = f32[4,256]{1,0:T(4,128)S(1)} copy-done((f32[4,256]{1,0:T(4,128)S(1)}, f32[4,256]{1,0:T(4,128)}, u32[]{:S(2)}) %copy-start.2) | copy-done | bytes 4120
  4.4 0.0 copy-start.3
  4.4 0.7 %copy-done.3 = f32[4,256]{1,0:T(4,128)S(1)} copy-done((f32[4,256]{1,0:T(4,128)S(1)}, f32[4,256]{1,0:T(4,128)}, u32[]{:S(2)}) %copy-start.3) | copy-done | bytes 4120
  5.0 45.3 %circuit.1 = f32[1024,128]{1,0:T(8,128)S(1)} custom-call(f32[1024,128]{1,0:T(8,128)S(1)} %bitcast.13, f32[48,128,128]{2,1,0:T(8,128)S(1)} %bitcast.11, f32[4,256]{1,0:T(4,128)S(1)} %copy-done.2, f32[4,256]{1,0:T(4,128)S(1)} %copy-done.3, f32[4,1,1]{2,1,0:T(1,128)S(1)} %copy.7.p_glob), custom_call_target="tpu_custom_call" | custom-call | tf_op jit(solution)/shard_map/circuit/pallas_call | solution.py:359
  50.3 0.8 %copy.10 = f32[2,65536]{1,0:T(2,128)} copy(f32[2,65536]{1,0:T(2,128)S(1)} %bitcast.12) | data formatting | bytes 1048576
Async XLA Ops:
  0.7 1.9 %copy-start = (f32[4,6,2,128,128]{4,3,2,1,0:T(8,128)S(1)}, f32[4,6,2,128,128]{4,3,2,1,0:T(8,128)}, u32[]{:S(2)}) copy-start(f32[4,6,2,128,128]{4,3,2,1,0:T(8,128)} %param.6) | copy-start | bytes 9437188
  2.6 1.0 %copy-start.1 = (f32[2,65536]{1,0:T(2,128)S(1)}, f32[2,65536]{1,0:T(2,128)}, u32[]{:S(2)}) copy-start(f32[2,65536]{1,0:T(2,128)} %param.5) | copy-start | bytes 1572868
  3.7 0.7 %copy-start.2 = (f32[4,256]{1,0:T(4,128)S(1)}, f32[4,256]{1,0:T(4,128)}, u32[]{:S(2)}) copy-start(f32[4,256]{1,0:T(4,128)} %p_low.1) | copy-start | bytes 12292
  4.4 0.7 %copy-start.3 = (f32[4,256]{1,0:T(4,128)S(1)}, f32[4,256]{1,0:T(4,128)}, u32[]{:S(2)}) copy-start(f32[4,256]{1,0:T(4,128)} %p_high.1) | copy-start | bytes 12292

commit v2 on v1

--- a/solution.py
+++ b/solution.py
@@ -75,8 +75,7 @@
     amp_copy.start()
     for copy in small:
         copy.start()
-    for s in range(1, 4):
-        gate_copies[s].start()
+    gate_copies[1].start()
 
     barrier = pltpu.get_barrier_semaphore()
 
@@ -224,10 +223,27 @@
         view = bufs.at[stage, k, pl.ds(0, moved)]
         pltpu.make_async_copy(view, view, sem.at[stage, k]).wait()
 
+    for copy in small:
+        copy.wait()
+    low_cos, low_sin = jnp.cos(low_v[...]), jnp.sin(low_v[...])
+    seg = iota((4, 256), 0)
+    glob = jnp.zeros((4, 256), F32)
+    for s in range(4):
+        glob = jnp.where(seg == s, glob_s[0, s], glob)
+    row_cos, row_sin = jnp.cos(high_v[...] + glob), jnp.sin(high_v[...] + glob)
+
+    def row_table(s):
+        c, t = expand(row_one_hot(), row_cos[s : s + 1], row_sin[s : s + 1])
+        row_t[s, 0] = c
+        row_t[s, 1] = part_sign((512, 128)) * t
+
+    row_table(0)
     gate_copies[0].wait()
+    amp_copy.wait()
+    gate_copies[1].wait()
+    gate_copies[2].start()
+    gate_copies[3].start()
     prepare(0, 0, 0, 2)
-    prepare_range(0, 1, 4)
-    amp_copy.wait()
     x = jnp.concatenate([amp_v[256 * u : 256 * u + 256, :] for u in range(4)], axis=1)
     y = dot3(wh[0], wl[0], x)
     for u in range(4):
@@ -235,37 +251,19 @@
             full[b7, u * 128 : u * 128 + 128] = y[
                 128 * b7 : 128 * b7 + 128, 128 * u : 128 * u + 128
             ]
+    prepare(0, 1, 1, 1)
     full_top(1)
+    prepare(0, 2, 0, 0)
+    prepare_low(0, 0, low_cos, low_sin)
     full_middle(2, full)
-
-    for copy in small:
-        copy.wait()
-    low_cos, low_sin = jnp.cos(low_v[...]), jnp.sin(low_v[...])
-    seg = iota((4, 256), 0)
-    glob = jnp.zeros((4, 256), F32)
-    for s in range(4):
-        glob = jnp.where(seg == s, glob_s[s, 0, 0], glob)
-    row_cos, row_sin = jnp.cos(high_v[...] + glob), jnp.sin(high_v[...] + glob)
-
-    def row_table(s):
-        c, t = expand(row_one_hot(), row_cos[s : s + 1], row_sin[s : s + 1])
-        row_t[s, 0] = c
-        row_t[s, 1] = part_sign((512, 128)) * t
-
-    row_table(0)
-    gate_copies[1].wait()
-    prepare_low(0, 0, low_cos, low_sin)
-    a, b = half_swap(apply_low(0, 0, full[0]), apply_low(0, 1, full[1]))
-    full[0] = a
-    full[1] = b
+    prepare(0, 3, 1, 1)
+    halves = half_swap(apply_low(0, 0, full[0]), apply_low(0, 1, full[1]))
+    y = dot3(wh[3], wl[3], jnp.concatenate([columns(h) for h in halves], axis=1))
+    for k in range(2):
+        sends[0, k] = turn(rows_again(y[:, 256 * k : 256 * k + 256]), row_t, 0)
     pl.semaphore_wait(barrier, 38)
-
-    def leave0(k, carry):
-        sends[0, k] = turn(top_gate(3, full[k]), row_t, 0)
+    for k in range(2):
         start(0, k, "qa", qa, 8)
-        return carry
-
-    lax.fori_loop(0, 2, leave0, 0)
 
     prepare_range(1, 0, 4)
     row_table(1)
@@ -359,7 +357,7 @@
     result = pl.pallas_call(
         kernel,
         name="circuit",
-        out_shape=jax.ShapeDtypeStruct((2 * rows, 128), F32),
+        out_shape=pltpu.VMEM((2 * rows, 128), F32),
         in_specs=[anywhere] * 5,
         out_specs=pl.BlockSpec(memory_space=pltpu.VMEM),
         scratch_shapes=[
@@ -367,7 +365,7 @@
             pltpu.VMEM((48, 128, 128), F32),
             pltpu.VMEM((4, 256), F32),
             pltpu.VMEM((4, 256), F32),
-            pltpu.SMEM((4, 1, 1), F32),
+            pltpu.SMEM((1, 4), F32),
             pltpu.VMEM((3, 256, 256), BF16),
             pltpu.VMEM((16, 256, 256), BF16),
             pltpu.VMEM((16, 256, 256), BF16),
@@ -385,9 +383,9 @@
             pltpu.SemaphoreType.DMA((3, 2)),
         ],
         compiler_params=pltpu.CompilerParams(
-            collective_id=0, has_side_effects=True, vmem_limit_bytes=40 << 20
+            collective_id=0, has_side_effects=True, vmem_limit_bytes=60 << 20
         ),
-    )(amp, gate_blocks.reshape(48, 128, 128), phase_low, phase_high, phase_global)
+    )(amp, gate_blocks.reshape(48, 128, 128), phase_low, phase_high, phase_global.reshape(1, 4))
     return result.reshape(rows, 2, 128).transpose(1, 0, 2).reshape(2, cells)
 
 

time: 51.4 us -> 45 us (0.88)
  local copies, waits for them, and re-layouts: 5.84 us -> 0.8 us
  Pallas kernels: 45.3 us -> 44.1 us
    unnamed x10 -> x1, local copies, waits for them, and re-layouts: 5.84 us -> 0.8 us
    pallas_call x1, Pallas kernels: 45.3 us -> 44.1 us  [body(): pl.pallas_call(kernel, name='circuit', out_shape=pltpu.VMEM((2 * rows, 12...]
where the time goes in v2:
time: 45 us; the launch traced here: 44.9 us
  Pallas kernels  44.1 us (98%)
  local copies, waits for them, and re-layouts  0.8 us (2%)
    pallas_call x1, Pallas kernels, body(): pl.pallas_call(kernel, name='circuit', out_shape=pltpu.VMEM((2 * rows, 12...  44.1 us

profile of v2, /device:TPU:1, one launch (start us, length us, event | category | flops | bytes accessed | tf_op | source)
XLA Modules:
  0.0 44.9 jit_solution(6823515267857996812)
XLA Ops:
  0.0 44.1 %circuit.1 = f32[1024,128]{1,0:T(8,128)S(1)} custom-call(f32[1024,128]{1,0:T(8,128)} %bitcast.14, f32[48,128,128]{2,1,0:T(8,128)} %bitcast.13, f32[4,256]{1,0:T(4,128)} %p_low.1, f32[4,256]{1,0:T(4,128)} %p_high.1, f32[1,4]{1,0:T(1,128)} %bitcast.15), custom_call_target="tpu_custom_call" | custom-call | tf_op jit(solution)/shard_map/circuit/pallas_call | solution.py:357
  44.1 0.8 %copy.9 = f32[2,65536]{1,0:T(2,128)} copy(f32[2,65536]{1,0:T(2,128)S(1)} %bitcast.12) | data formatting | bytes 1048576

commit v3 on v2

--- a/solution.py
+++ b/solution.py
@@ -203,7 +203,7 @@
         size = 512 // count
 
         def step(i, carry):
-            peer = lax.rem(me + i, count)
+            peer = lax.rem(me + i, count) if axis == "qa" else i - 1 + jnp.where(i > me, 1, 0)
             pltpu.make_async_remote_copy(
                 src_ref=sends.at[stage, k, pl.ds(pl.multiple_of(peer * size, size), size)],
                 dst_ref=recvs.at[stage, k, pl.ds(pl.multiple_of(me * size, size), size)],

time: 45 us -> 43.6 us (0.969)
  Pallas kernels: 44.1 us -> 42.7 us
    pallas_call x1, Pallas kernels: 44.1 us -> 42.7 us  [body(): pl.pallas_call(kernel, name='circuit', out_shape=pltpu.VMEM((2 * rows, 12...]
where the time goes in v3:
time: 43.6 us; the launch traced here: 43.5 us
  Pallas kernels  42.7 us (98%)
  local copies, waits for them, and re-layouts  0.8 us (2%)
    pallas_call x1, Pallas kernels, body(): pl.pallas_call(kernel, name='circuit', out_shape=pltpu.VMEM((2 * rows, 12...  42.7 us

profile of v3, /device:TPU:1, one launch (start us, length us, event | category | flops | bytes accessed | tf_op | source)
XLA Modules:
  0.0 43.5 jit_solution(4222568179164827289)
XLA Ops:
  0.0 42.7 %circuit.1 = f32[1024,128]{1,0:T(8,128)S(1)} custom-call(f32[1024,128]{1,0:T(8,128)} %bitcast.14, f32[48,128,128]{2,1,0:T(8,128)} %bitcast.13, f32[4,256]{1,0:T(4,128)} %p_low.1, f32[4,256]{1,0:T(4,128)} %p_high.1, f32[1,4]{1,0:T(1,128)} %bitcast.15), custom_call_target="tpu_custom_call" | custom-call | tf_op jit(solution)/shard_map/circuit/pallas_call | solution.py:357
  42.7 0.8 %copy.9 = f32[2,65536]{1,0:T(2,128)} copy(f32[2,65536]{1,0:T(2,128)S(1)} %bitcast.12) | data formatting | bytes 1048576

commit v4 on v3

--- a/solution.py
+++ b/solution.py
@@ -313,7 +313,7 @@
         finish(recvs, recv_sem, 1, k, 32)
         x = middle_gate(8, recvs[1, k])
         x = top_gate(9, x)
-        full[k] = middle_gate(10, x)
+        full[k] = turn(top_gate(11, middle_gate(10, x)), row_t, 2)
         return carry
 
     lax.fori_loop(0, 2, arrive1, 0)
@@ -322,8 +322,7 @@
     full[1] = b
 
     def leave2(b7, carry):
-        x = apply_low(1, b7, full[b7])
-        sends[2, b7] = turn(top_gate(11, x), row_t, 2)
+        sends[2, b7] = apply_low(1, b7, full[b7])
         start(2, b7, "qa", qa, 8)
         return carry
 

time: 43.6 us -> 43.6 us (level)
  no operation moved by 1% of the time
where the time goes in v4:
time: 43.6 us; the launch traced here: 43.5 us
  Pallas kernels  42.7 us (98%)
  local copies, waits for them, and re-layouts  0.8 us (2%)
    pallas_call x1, Pallas kernels, body(): pl.pallas_call(kernel, name='circuit', out_shape=pltpu.VMEM((2 * rows, 12...  42.7 us

profile of v4, /device:TPU:1, one launch (start us, length us, event | category | flops | bytes accessed | tf_op | source)
XLA Modules:
  0.0 43.5 jit_solution(5381650343388454429)
XLA Ops:
  0.0 42.7 %circuit.1 = f32[1024,128]{1,0:T(8,128)S(1)} custom-call(f32[1024,128]{1,0:T(8,128)} %bitcast.14, f32[48,128,128]{2,1,0:T(8,128)} %bitcast.13, f32[4,256]{1,0:T(4,128)} %p_low.1, f32[4,256]{1,0:T(4,128)} %p_high.1, f32[1,4]{1,0:T(1,128)} %bitcast.15), custom_call_target="tpu_custom_call" | custom-call | tf_op jit(solution)/shard_map/circuit/pallas_call | solution.py:356
  42.7 0.8 %copy.9 = f32[2,65536]{1,0:T(2,128)} copy(f32[2,65536]{1,0:T(2,128)S(1)} %bitcast.12) | data formatting | bytes 1048576

commit v5 on v4

--- a/solution.py
+++ b/solution.py
@@ -60,10 +60,8 @@
     qa, qb = lax.axis_index("qa"), lax.axis_index("qb")
 
     gate_copies = [
-        pltpu.make_async_copy(
-            gates.at[pl.ds(12 * s, 12)], gates_v.at[pl.ds(12 * s, 12)], gate_sem.at[s]
-        )
-        for s in range(4)
+        pltpu.make_async_copy(gates.at[pl.ds(at, n)], gates_v.at[pl.ds(at, n)], gate_sem.at[i])
+        for i, (at, n) in enumerate(((2, 2), (4, 8), (0, 2), (12, 12), (24, 24)))
     ]
     amp_copy = pltpu.make_async_copy(amp, amp_v, in_sem.at[0])
     small = [
@@ -71,11 +69,8 @@
         pltpu.make_async_copy(p_high, high_v, in_sem.at[2]),
         pltpu.make_async_copy(p_glob, glob_s, in_sem.at[3]),
     ]
-    gate_copies[0].start()
-    amp_copy.start()
-    for copy in small:
+    for copy in small + [gate_copies[0], amp_copy] + gate_copies[1:4]:
         copy.start()
-    gate_copies[1].start()
 
     barrier = pltpu.get_barrier_semaphore()
 
@@ -240,9 +235,6 @@
     row_table(0)
     gate_copies[0].wait()
     amp_copy.wait()
-    gate_copies[1].wait()
-    gate_copies[2].start()
-    gate_copies[3].start()
     prepare(0, 0, 0, 2)
     x = jnp.concatenate([amp_v[256 * u : 256 * u + 256, :] for u in range(4)], axis=1)
     y = dot3(wh[0], wl[0], x)
@@ -251,6 +243,9 @@
             full[b7, u * 128 : u * 128 + 128] = y[
                 128 * b7 : 128 * b7 + 128, 128 * u : 128 * u + 128
             ]
+    for copy in gate_copies[1:4]:
+        copy.wait()
+    gate_copies[4].start()
     prepare(0, 1, 1, 1)
     full_top(1)
     prepare(0, 2, 0, 0)
@@ -291,8 +286,7 @@
 
     lax.fori_loop(0, 2, between, 0)
 
-    gate_copies[2].wait()
-    gate_copies[3].wait()
+    gate_copies[4].wait()
     prepare_range(2, 0, 4)
     prepare_range(3, 0, 3)
     prepare(3, 3, None, 1)
@@ -377,7 +371,7 @@
             pltpu.VMEM((2, 2, 512, 128), F32),
             pltpu.VMEM((2, 2, 2, 128, 128), F32),
             pltpu.SemaphoreType.DMA((4,)),
-            pltpu.SemaphoreType.DMA((4,)),
+            pltpu.SemaphoreType.DMA((5,)),
             pltpu.SemaphoreType.DMA((3, 2)),
             pltpu.SemaphoreType.DMA((3, 2)),
         ],

time: 43.6 us -> 43.7 us (level)
  no operation moved by 1% of the time
where the time goes in v5:
time: 43.7 us; the launch traced here: 43.4 us
  Pallas kernels  42.6 us (97%)
  local copies, waits for them, and re-layouts  0.8 us (2%)
    pallas_call x1, Pallas kernels, body(): pl.pallas_call(kernel, name='circuit', out_shape=pltpu.VMEM((2 * rows, 12...  42.6 us

profile of v5, /device:TPU:1, one launch (start us, length us, event | category | flops | bytes accessed | tf_op | source)
XLA Modules:
  0.0 43.4 jit_solution(14808540810925392403)
XLA Ops:
  0.0 42.6 %circuit.1 = f32[1024,128]{1,0:T(8,128)S(1)} custom-call(f32[1024,128]{1,0:T(8,128)} %bitcast.14, f32[48,128,128]{2,1,0:T(8,128)} %bitcast.13, f32[4,256]{1,0:T(4,128)} %p_low.1, f32[4,256]{1,0:T(4,128)} %p_high.1, f32[1,4]{1,0:T(1,128)} %bitcast.15), custom_call_target="tpu_custom_call" | custom-call | tf_op jit(solution)/shard_map/circuit/pallas_call | solution.py:350
  42.6 0.8 %copy.9 = f32[2,65536]{1,0:T(2,128)} copy(f32[2,65536]{1,0:T(2,128)S(1)} %bitcast.12) | data formatting | bytes 1048576
